TPU v7x, 32 devices: a whole 2x2x4 slice. The times are simulated.
32 devices in a mesh: sp: 8 (over z, x), wa: 4 (over y, core).
Axes of the slice: x: 2, y: 2, z: 4, core: 2. Of those that a mesh axis runs over, the one named last changes fastest.
Arguments:
- fields_in: bfloat16 [2, 24, 180, 768], P(None, 'sp'), may hold values from -6 to 6
- norm1_gain: float32 [768], replicated, may hold values from 0.1 to 1.9
- norm1_shift: float32 [768], replicated, may hold values from -1.75 to 1.75
- spec_w1: bfloat16 [8, 2, 96, 96], P('wa'), may hold values from -0.4375 to 0.4375
- spec_b1: bfloat16 [8, 2, 96], P('wa'), may hold values from -0.625 to 0.625
- spec_w2: bfloat16 [8, 2, 96, 96], P('wa'), may hold values from -0.4375 to 0.4375
- spec_b2: bfloat16 [8, 2, 96], P('wa'), may hold values from -0.625 to 0.625
- norm2_gain: float32 [768], replicated, may hold values from 0.1 to 1.9
- norm2_shift: float32 [768], replicated, may hold values from -1.75 to 1.75
- fc1_weight: bfloat16 [768, 3072], P(None, 'wa'), may hold values from -0.21875 to 0.21875
- fc1_bias: bfloat16 [3072], P('wa'), may hold values from -1.75 to 1.75
- fc2_weight: bfloat16 [3072, 768], P('wa'), may hold values from -0.109375 to 0.109375
- fc2_bias: bfloat16 [768], replicated, may hold values from -1.75 to 1.75
- out_grad: bfloat16 [2, 24, 180, 768], P(None, 'sp'), may hold values from -6 to 6
Outputs:
- output: float32 [2, 24, 180, 768], P(None, 'sp')
- fields_grad: float32 [2, 24, 180, 768], P(None, 'sp')
- norm1_gain_grad: float32 [768], replicated
- norm1_shift_grad: float32 [768], replicated
- spec_w1_grad: float32 [8, 2, 96, 96], P('wa')
- spec_b1_grad: float32 [8, 2, 96], P('wa')
- spec_w2_grad: float32 [8, 2, 96, 96], P('wa')
- spec_b2_grad: float32 [8, 2, 96], P('wa')
- norm2_gain_grad: float32 [768], replicated
- norm2_shift_grad: float32 [768], replicated
- fc1_weight_grad: float32 [768, 3072], P(None, 'wa')
- fc1_bias_grad: float32 [3072], P('wa')
- fc2_weight_grad: float32 [3072, 768], P('wa')
- fc2_bias_grad: float32 [768], replicated
All inputs are finite; a program needn't handle non-finite values.
Results may differ from a plain program's by a relative error of at most 0.024.
The roundings to bfloat16 on the way count: a program that leaves them out, or rounds other values in their place, can miss the bound.
Values may be sent and summed in bfloat16 or wider, within the bound.
A program may use at most 128 MiB of HBM per device.

v0:
```python
import math

import jax
import jax.numpy as jnp
from jax import lax
from jax.sharding import PartitionSpec as P

threshold = 0.01


def phase_angles(rows, columns, period):
    product = rows[:, None] * columns[None, :] % period
    return 2.0 * math.pi / period * product.astype(jnp.float32)


def width_tables(width, modes):
    positions = jnp.arange(width, dtype=jnp.int32)
    wavenums = jnp.arange(modes, dtype=jnp.int32)
    angles = phase_angles(positions, wavenums, width)
    scale = 1.0 / math.sqrt(width)
    cosine = jnp.cos(angles)
    sine = jnp.sin(angles)
    forward_cos = cosine * scale
    forward_sin = -sine * scale
    weights = jnp.where((wavenums == 0) | (2 * wavenums == width), 1.0, 2.0).astype(jnp.float32)
    inverse_cos = weights[:, None] * cosine.T * scale
    inverse_sin = -(weights[:, None] * sine.T) * scale
    return (forward_cos, forward_sin, inverse_cos, inverse_sin)


def height_tables(modes, rows, period):
    angles = phase_angles(modes, rows, period)
    scale = 1.0 / math.sqrt(period)
    cosine = (jnp.cos(angles) * scale).astype(jnp.bfloat16)
    sine = (jnp.sin(angles) * scale).astype(jnp.bfloat16)
    return (cosine, sine)


def swap_forward(values):
    half = values.shape[-1] // 2
    return jnp.concatenate([values[..., half:], -values[..., :half]], -1)


def swap_inverse(values):
    half = values.shape[-1] // 2
    return jnp.concatenate([-values[..., half:], values[..., :half]], -1)


def modes_from_rows(rows_data, mode_index, row_index, period):
    cosine, sine = height_tables(mode_index, row_index, period)
    first = jnp.einsum("qh,hfkc->qfkc", cosine, rows_data, preferred_element_type=jnp.float32)
    return first + jnp.einsum(
        "qh,hfkc->qfkc", sine, swap_forward(rows_data), preferred_element_type=jnp.float32
    )


def rows_from_modes(mode_data, row_index, mode_index, period):
    cosine, sine = height_tables(mode_index, row_index, period)
    first = jnp.einsum("qh,qfkc->hfkc", cosine, mode_data, preferred_element_type=jnp.float32)
    return first + jnp.einsum(
        "qh,qfkc->hfkc", sine, swap_inverse(mode_data), preferred_element_type=jnp.float32
    )


def modes_term(rows_data, own_index, period, count):
    return modes_from_rows(rows_data, jnp.arange(count, dtype=jnp.int32), own_index, period)


def rows_term(mode_data, own_index, period, count):
    return rows_from_modes(mode_data, jnp.arange(count, dtype=jnp.int32), own_index, period)


def split_blocks(values, blocks):
    half = values.shape[-1] // 2
    shape = values.shape[:-1] + (blocks, half // blocks)
    return (values[..., :half].reshape(shape), values[..., half:].reshape(shape))


def join_blocks(real_part, imag_part):
    leading = real_part.shape[:-2]
    return jnp.concatenate(
        [real_part.reshape(leading + (-1,)), imag_part.reshape(leading + (-1,))], -1
    )


def block_product(left, right):
    return jnp.einsum("qfkbc,bcd->qfkbd", left, right, preferred_element_type=jnp.float32)


def block_transposed(left, right):
    return jnp.einsum("qfkbd,bcd->qfkbc", left, right, preferred_element_type=jnp.float32)


def block_outer(left, right):
    return jnp.einsum("qfkbc,qfkbd->bcd", left, right, preferred_element_type=jnp.float32)


def complex_apply(real_part, imag_part, weight_real, weight_imag):
    real_out = block_product(real_part, weight_real) - block_product(imag_part, weight_imag)
    imag_out = block_product(imag_part, weight_real) + block_product(real_part, weight_imag)
    return (real_out, imag_out)


def complex_adjoint(grad_real, grad_imag, weight_real, weight_imag):
    real_in = block_transposed(grad_real, weight_real) + block_transposed(grad_imag, weight_imag)
    imag_in = block_transposed(grad_imag, weight_real) - block_transposed(grad_real, weight_imag)
    return (real_in, imag_in)


def complex_weight_grads(real_part, imag_part, grad_real, grad_imag):
    weight_real = block_outer(real_part, grad_real) + block_outer(imag_part, grad_imag)
    weight_imag = block_outer(real_part, grad_imag) - block_outer(imag_part, grad_real)
    bias_real = jnp.sum(grad_real, (0, 1, 2), dtype=jnp.float32)
    bias_imag = jnp.sum(grad_imag, (0, 1, 2), dtype=jnp.float32)
    return (jnp.stack([weight_real, weight_imag], 1), jnp.stack([bias_real, bias_imag], 1))


def layer_norm(values, gain, shift):
    centred = values - jnp.mean(values, -1, keepdims=True)
    variance = jnp.mean(centred * centred, -1, keepdims=True)
    inv_std = lax.rsqrt(variance + 1e-05)
    normal_hat = centred * inv_std
    return (normal_hat * gain + shift, normal_hat, inv_std)


def norm_backward(grad, normal_hat, inv_std, gain):
    scaled = grad * gain
    return inv_std * (
        scaled
        - jnp.mean(scaled, -1, keepdims=True)
        - normal_hat * jnp.mean(scaled * normal_hat, -1, keepdims=True)
    )


def shrink(values):
    return values - threshold * jnp.tanh(values / threshold)


def shrink_slope(values):
    bent = jnp.tanh(values / threshold)
    return bent * bent


def local(
    fields_in,
    norm1_gain,
    norm1_shift,
    spec_w1,
    spec_b1,
    spec_w2,
    spec_b2,
    norm2_gain,
    norm2_shift,
    fc1_weight,
    fc1_bias,
    fc2_weight,
    fc2_bias,
    out_grad,
):
    fields, rows_here, width, channels = fields_in.shape
    blocks_here = spec_w1.shape[0]
    share = blocks_here * spec_w1.shape[2]
    modes = width // 2 + 1
    period = rows_here * lax.axis_size("sp")
    own_index = lax.axis_index("sp") * rows_here + jnp.arange(rows_here, dtype=jnp.int32)
    block_start = lax.axis_index("wa") * share
    tables = width_tables(width, modes)
    forward_cos, forward_sin, inverse_cos, inverse_sin = [
        table.astype(jnp.bfloat16) for table in tables
    ]
    all_but_last = (0, 1, 2)
    input_wide = fields_in.astype(jnp.float32)
    normed_one, hat_one, inv_std_one = layer_norm(input_wide, norm1_gain, norm1_shift)
    own_channels = lax.dynamic_slice_in_dim(normed_one.astype(jnp.bfloat16), block_start, share, 3)
    col_real = jnp.einsum(
        "fhwc,wk->hfkc", own_channels, forward_cos, preferred_element_type=jnp.float32
    )
    col_imag = jnp.einsum(
        "fhwc,wk->hfkc", own_channels, forward_sin, preferred_element_type=jnp.float32
    )
    column_modes = jnp.concatenate([col_real, col_imag], -1).astype(jnp.bfloat16)
    spectrum = lax.psum_scatter(
        modes_term(column_modes, own_index, period, lax.axis_size("sp") * rows_here),
        "sp",
        scatter_dimension=0,
        tiled=True,
    )
    spec_real, spec_imag = split_blocks(spectrum.astype(jnp.bfloat16), blocks_here)
    one_real, one_imag = complex_apply(spec_real, spec_imag, spec_w1[:, 0], spec_w1[:, 1])
    one_real = one_real + spec_b1[:, 0].astype(jnp.float32)
    one_imag = one_imag + spec_b1[:, 1].astype(jnp.float32)
    hid_real, real_pull = jax.vjp(jax.nn.gelu, one_real)
    hid_imag, imag_pull = jax.vjp(jax.nn.gelu, one_imag)
    hid_real = hid_real.astype(jnp.bfloat16)
    hid_imag = hid_imag.astype(jnp.bfloat16)
    two_real, two_imag = complex_apply(hid_real, hid_imag, spec_w2[:, 0], spec_w2[:, 1])
    two_real = two_real + spec_b2[:, 0].astype(jnp.float32)
    two_imag = two_imag + spec_b2[:, 1].astype(jnp.float32)
    filtered = join_blocks(shrink(two_real), shrink(two_imag)).astype(jnp.bfloat16)
    row_spectrum = lax.psum_scatter(
        rows_term(filtered, own_index, period, lax.axis_size("sp") * rows_here),
        "sp",
        scatter_dimension=0,
        tiled=True,
    )
    row_spectrum = row_spectrum.astype(jnp.bfloat16)
    filter_own = jnp.einsum(
        "hfkc,kw->fhwc", row_spectrum[..., :share], inverse_cos, preferred_element_type=jnp.float32
    )
    filter_own = filter_own + jnp.einsum(
        "hfkc,kw->fhwc", row_spectrum[..., share:], inverse_sin, preferred_element_type=jnp.float32
    )
    filter_all = lax.all_gather(filter_own.astype(jnp.bfloat16), "wa", axis=3, tiled=True)
    mixed = input_wide + filter_all.astype(jnp.float32)
    normed_two, hat_two, inv_std_two = layer_norm(mixed, norm2_gain, norm2_shift)
    normed_rows = normed_two.astype(jnp.bfloat16).reshape(-1, channels)
    hidden_pre = jnp.dot(
        normed_rows, fc1_weight, preferred_element_type=jnp.float32
    ) + fc1_bias.astype(jnp.float32)
    activated, gelu_pull = jax.vjp(jax.nn.gelu, hidden_pre)
    activated = activated.astype(jnp.bfloat16)
    branch = lax.psum(jnp.dot(activated, fc2_weight, preferred_element_type=jnp.float32), "wa")
    output = mixed + (branch + fc2_bias.astype(jnp.float32)).reshape(mixed.shape)
    grad_rows = out_grad.reshape(-1, channels)
    fc2_weight_grad = jnp.einsum(
        "re,rd->ed", activated, grad_rows, preferred_element_type=jnp.float32
    )
    fc2_bias_grad = jnp.sum(grad_rows, 0, dtype=jnp.float32)
    grad_act = jnp.einsum("rd,ed->re", grad_rows, fc2_weight, preferred_element_type=jnp.float32)
    grad_hidden = gelu_pull(grad_act)[0].astype(jnp.bfloat16)
    fc1_weight_grad = jnp.einsum(
        "rd,re->de", normed_rows, grad_hidden, preferred_element_type=jnp.float32
    )
    fc1_bias_grad = jnp.sum(grad_hidden, 0, dtype=jnp.float32)
    grad_norm_part = jnp.einsum(
        "re,de->rd", grad_hidden, fc1_weight, preferred_element_type=jnp.float32
    )
    grad_norm_two = lax.psum(grad_norm_part, "wa").reshape(mixed.shape)
    norm2_gain_grad = jnp.sum(grad_norm_two * hat_two, all_but_last)
    norm2_shift_grad = jnp.sum(grad_norm_two, all_but_last)
    grad_mixed = out_grad.astype(jnp.float32) + norm_backward(
        grad_norm_two, hat_two, inv_std_two, norm2_gain
    )
    grad_filter = lax.dynamic_slice_in_dim(grad_mixed, block_start, share, 3).astype(jnp.bfloat16)
    grad_back_real = jnp.einsum(
        "fhwc,kw->hfkc", grad_filter, inverse_cos, preferred_element_type=jnp.float32
    )
    grad_back_imag = jnp.einsum(
        "fhwc,kw->hfkc", grad_filter, inverse_sin, preferred_element_type=jnp.float32
    )
    grad_back = jnp.concatenate([grad_back_real, grad_back_imag], -1).astype(jnp.bfloat16)
    grad_filtered = lax.psum_scatter(
        modes_term(grad_back, own_index, period, lax.axis_size("sp") * rows_here),
        "sp",
        scatter_dimension=0,
        tiled=True,
    )
    grad_out_real, grad_out_imag = split_blocks(grad_filtered, blocks_here)
    grad_two_real = (grad_out_real * shrink_slope(two_real)).astype(jnp.bfloat16)
    grad_two_imag = (grad_out_imag * shrink_slope(two_imag)).astype(jnp.bfloat16)
    spec_w2_grad, spec_b2_grad = complex_weight_grads(
        hid_real, hid_imag, grad_two_real, grad_two_imag
    )
    grad_hid_real, grad_hid_imag = complex_adjoint(
        grad_two_real, grad_two_imag, spec_w2[:, 0], spec_w2[:, 1]
    )
    grad_one_real = real_pull(grad_hid_real)[0].astype(jnp.bfloat16)
    grad_one_imag = imag_pull(grad_hid_imag)[0].astype(jnp.bfloat16)
    spec_w1_grad, spec_b1_grad = complex_weight_grads(
        spec_real, spec_imag, grad_one_real, grad_one_imag
    )
    grad_spec_real, grad_spec_imag = complex_adjoint(
        grad_one_real, grad_one_imag, spec_w1[:, 0], spec_w1[:, 1]
    )
    grad_spectrum = join_blocks(grad_spec_real, grad_spec_imag).astype(jnp.bfloat16)
    grad_columns = lax.psum_scatter(
        rows_term(grad_spectrum, own_index, period, lax.axis_size("sp") * rows_here),
        "sp",
        scatter_dimension=0,
        tiled=True,
    )
    grad_columns = grad_columns.astype(jnp.bfloat16)
    grad_norm_own = jnp.einsum(
        "hfkc,wk->fhwc", grad_columns[..., :share], forward_cos, preferred_element_type=jnp.float32
    )
    grad_norm_own = grad_norm_own + jnp.einsum(
        "hfkc,wk->fhwc", grad_columns[..., share:], forward_sin, preferred_element_type=jnp.float32
    )
    grad_norm_one = lax.all_gather(
        grad_norm_own.astype(jnp.bfloat16), "wa", axis=3, tiled=True
    ).astype(jnp.float32)
    norm1_gain_grad = jnp.sum(grad_norm_one * hat_one, all_but_last)
    norm1_shift_grad = jnp.sum(grad_norm_one, all_but_last)
    fields_grad = grad_mixed + norm_backward(grad_norm_one, hat_one, inv_std_one, norm1_gain)
    summed = lax.psum(
        (
            fc1_weight_grad,
            fc1_bias_grad,
            fc2_weight_grad,
            fc2_bias_grad,
            spec_w1_grad,
            spec_b1_grad,
            spec_w2_grad,
            spec_b2_grad,
            norm1_gain_grad,
            norm1_shift_grad,
            norm2_gain_grad,
            norm2_shift_grad,
        ),
        "sp",
    )
    return (
        output,
        fields_grad,
        summed[8],
        summed[9],
        summed[4],
        summed[5],
        summed[6],
        summed[7],
        summed[10],
        summed[11],
        summed[0],
        summed[1],
        summed[2],
        summed[3],
    )


def solution(mesh):
    return jax.shard_map(
        local,
        mesh=mesh,
        in_specs=(
            P(None, "sp", None, None),
            P(),
            P(),
            P("wa", None, None, None),
            P("wa", None, None),
            P("wa", None, None, None),
            P("wa", None, None),
            P(),
            P(),
            P(None, "wa"),
            P("wa"),
            P("wa", None),
            P(),
            P(None, "sp", None, None),
        ),
        out_specs=(
            P(None, "sp", None, None),
            P(None, "sp", None, None),
            P(),
            P(),
            P("wa", None, None, None),
            P("wa", None, None),
            P("wa", None, None, None),
            P("wa", None, None),
            P(),
            P(),
            P(None, "wa"),
            P("wa"),
            P("wa", None),
            P(),
        ),
        check_vma=False,
    )
```

profile of v0, /device:TPU:0, one launch (start us, length us, event | category | flops | bytes accessed | tf_op | source)
XLA Modules:
  0.0 1590.4 jit_solution(6406376452412865366)
XLA Ops:
  9.0 1.7 convert_reduce_fusion.1
  10.7 2.1 fusion.5
  13.3 1.6 fusion.39
  17.0 1.4 pad_maximum_fusion.1
  19.6 4.1 convolution_add_fusion.4
  23.7 9.1 copy.197
  32.8 265.9 %all-reduce.19 = bf16[24,2,91,384]{3,1,2,0:T(2,128)(2,1)} all-reduce(f32[24,2,91,384]{3,1,2,0:T(2,128)} %copy.197), channel_id=2, replica_groups=mesh['sp'=8,'wa'=4] {'sp'}, use_global_device_ids=true, to_apply=%region_2.3.clone | all-reduce | flops 1677312 | bytes 10063872
  306.3 2.2 multiply_convert_fusion.3
  315.6 2.0 subtract_convert_fusion
  322.0 1.7 pad_maximum_fusion.4
  323.6 2.5 fusion.66
  326.1 4.1 convolution_add_fusion.3
  330.2 9.1 copy.215
  339.3 263.3 %all-reduce.20 = bf16[24,2,91,384]{3,1,2,0:T(2,128)(2,1)} all-reduce(f32[24,2,91,384]{3,1,2,0:T(2,128)} %copy.215), channel_id=3, replica_groups=mesh['sp'=8,'wa'=4] {'sp'}, use_global_device_ids=true, to_apply=%region_3.4.clone | all-reduce | flops 1677312 | bytes 10063872
  604.6 1.5 fusion.33
  606.1 2.1 copy.217
  608.3 2.8 copy.219
  611.2 3.6 reshape.171
  614.8 5.3 fusion.267
  620.1 11.3 all-gather.3.cloned.1.call-done
  631.4 6.6 copy.218
  638.0 2.0 fusion.19
  640.8 2.0 add_convert_fusion
  642.8 3.6 reshape.169
  646.4 6.8 convert_reduce_fusion.3
  653.2 3.8 fusion.261
  657.0 3.3 fusion.268
  660.9 125.0 %all-reduce.18.cloned.1.call-done = (f32[1080,768]{1,0:T(8,128)}, f32[1080,768]{1,0:T(8,128)}) async-done(((f32[1080,768]{1,0:T(8,128)}, f32[1080,768]{1,0:T(8,128)}), (f32[1080,768]{1,0:T(8,128)}, f32[1080,768]{1,0:T(8,128)})) %all-reduce.18.cloned.1.call-update) | async-done | bytes 6635536 | tf_op jit(solution)/shard_map/psum | solution.py:222
  786.0 4.8 reshape.172
  790.7 5.2 fusion.262
  796.1 3.2 multiply_reduce_fusion
  799.2 4.6 reshape.170
  803.8 6.7 convert_add_fusion.1
  813.6 4.1 convolution_add_fusion.2
  817.7 9.1 copy.223
  827.3 224.7 %all-reduce.14.cloned.1.call-done = f32[24,2,91,384]{3,1,2,0:T(2,128)} async-done(((f32[24,2,91,384]{3,1,2,0:T(2,128)}), f32[24,2,91,384]{3,1,2,0:T(2,128)}) %all-reduce.14.cloned.1.call-update) | async-done | bytes 6709264
  1052.1 3.0 constant_dynamic-slice_fusion
  1057.4 1.8 convert_reduce_fusion.5
  1060.3 2.1 copy.226
  1062.4 1.3 copy.227
  1063.7 1.9 convert_reduce_fusion.4
  1065.9 2.2 convert_reduce_fusion.6
  1079.2 1.7 pad_maximum_fusion.5
  1080.8 2.5 fusion.70
  1083.3 4.1 convolution_add_fusion.1
  1087.4 9.1 copy.235
  1096.5 263.8 %all-reduce.21 = bf16[24,2,91,384]{3,1,2,0:T(2,128)(2,1)} all-reduce(f32[24,2,91,384]{3,1,2,0:T(2,128)} %copy.235), channel_id=5, replica_groups=mesh['sp'=8,'wa'=4] {'sp'}, use_global_device_ids=true, to_apply=%region_11.12.clone | all-reduce | flops 1677312 | bytes 10063872
  1362.2 1.5 fusion.32
  1363.7 2.1 copy.237
  1367.1 1.9 copy.292
  1369.0 5.4 fusion.269
  1374.4 3.5 fusion.260
  1381.7 5.4 copy.255
  1387.1 1.8 all-gather.5.cloned.1.call-done
  1388.9 6.6 copy.238
  1395.5 3.1 fusion.10
  1398.7 2.7 fusion.8
  1401.5 3.4 copy.256
  1404.9 39.9 %all-reduce.4 = (f32[768]{0:T(1024)}, f32[768]{0:T(1024)}, f32[2,2,96]{2,1,0:T(2,128)}, f32[2,2,96]{2,1,0:T(2,128)}, f32[768]{0:T(1024)}, /*index=5*/f32[768]{0:T(1024)}, f32[768]{0:T(1024)}, f32[768]{0:T(1024)}) all-reduce(f32[768]{0:T(1024)S(1)} %get-tuple-element.72, ...), channel_id=1, replica_groups=mesh['sp'=8,'wa'=4] {'sp'}, use_global_device_ids=true, to_apply=%region_15.16 | all-reduce | flops 5376 | bytes 43008 | tf_op jit(solution)/shard_map/psum | solution.py:295
  1444.8 130.8 %all-reduce.16.cloned.1.call-done = (f32[2,2,96,96]{3,2,0,1:T(8,128)}, f32[2,2,96,96]{3,2,0,1:T(8,128)}, f32[768,768]{1,0:T(8,128)}, f32[768,768]{1,0:T(8,128)}) async-done(((f32[2,2,96,96]{3,2,0,1:T(8,128)}, f32[2,2,96,96]{3,2,0,1:T(8,128)}, f32[768,768]{1,0:T(8,128)}, f32[768,768]{1,0:T(8,128)}), (f32[2,2,96,96]{3,2,0,1:T(8,128)}, f32[2,2,96,96]{3,2,0,1:T(8,128)}, f32[768,768]{1,0:T(8,128)}, ...) | async-done | bytes 5013520 | tf_op jit(solution)/shard_map/psum | solution.py:295
  1575.6 1.8 copy.257
  1577.4 1.6 copy.258
  1579.0 3.3 copy.383
  1582.3 1.4 copy.384
  (174 shorter events, 52.6 us)
Async XLA Ops:
  7.2 639.2 %copy-start = (bf16[768,768]{1,0:T(8,128)(2,1)S(1)}, bf16[768,768]{1,0:T(8,128)(2,1)}, u32[]{:S(2)}) copy-start(bf16[768,768]{1,0:T(8,128)(2,1)} %param.23) | copy-start | bytes 3538948
  7.2 5.6 copy-start.2
  7.2 624.2 %all-gather.3.cloned.1.call-start = ((), (), s32[]{:S(2)}) async-start(), calls=%async_computation | async-start | bytes 2949120 | tf_op jit(solution)/shard_map/all_gather | solution.py:213
  7.3 597.3 %copy-start.22 = (f32[91]{0:T(128)}, f32[91]{0:T(128)S(1)}, u32[]{:S(2)}) copy-start(f32[91]{0:T(128)S(1)} %or_select_fusion) | copy-start | bytes 1096
  12.8 3.0 copy-start.28
  12.8 3.6 copy-start.29
  32.8 265.9 %copy-start.38 = (u32[32]{0:T(128)S(1)}, u32[32]{0:T(128)}, u32[]{:S(2)}) copy-start(u32[32]{0:T(128)} %constant.115) | copy-start | bytes 388
  32.8 270.9 %copy-start.15 = (bf16[2,2,96,96]{3,2,1,0:T(8,128)(2,1)S(1)}, bf16[2,2,96,96]{3,2,1,0:T(8,128)(2,1)}, u32[]{:S(2)}) copy-start(bf16[2,2,96,96]{3,2,1,0:T(8,128)(2,1)} %param.17) | copy-start | bytes 221188
  298.8 7.6 copy-start.36
  300.0 8.6 copy-start.35
  301.9 6.7 copy-start.7
  301.9 6.7 copy-start.8
  303.8 4.9 copy-start.14
  303.8 6.1 copy-start.16
  303.8 6.4 copy-start.26
  308.6 2.7 copy-start.12
  602.6 5.7 copy-start.31
  608.2 177.7 %all-reduce.18.cloned.1.call-start = ((), (), s32[]{:S(2)}) async-start(), calls=%async_computation.4 | async-start | bytes 13271040 | tf_op jit(solution)/shard_map/psum | solution.py:222
  638.0 2.0 copy-start.3
  638.0 2.8 copy-start.19
  638.0 2.8 copy-start.30
  646.4 6.8 copy-start.37
  653.1 3.8 copy-start.40
  653.2 3.8 copy-start.42
  660.3 0.7 copy-start.32
  660.3 391.8 %all-reduce.14.cloned.1.call-start = ((), (), s32[]{:S(2)}) async-start(), calls=%async_computation.2 | async-start | bytes 13418496
  803.8 6.7 copy-start.23
  810.5 1.9 copy-start.4
  826.9 230.6 %copy-start.9 = (f32[3,2,91,2,96]{4,2,1,0,3:T(8,128)S(1)}, f32[3,2,91,2,96]{4,2,1,0,3:T(8,128)}, u32[]{:S(2)}) copy-start(f32[3,2,91,2,96]{4,2,1,0,3:T(8,128)} %get-tuple-element.122) | copy-start | bytes 1257988
  826.9 232.3 %copy-start.17 = (bf16[2,2,96,96]{3,2,1,0:T(8,128)(2,1)S(1)}, bf16[2,2,96,96]{3,2,1,0:T(8,128)(2,1)}, u32[]{:S(2)}) copy-start(bf16[2,2,96,96]{3,2,1,0:T(8,128)(2,1)} %param.19) | copy-start | bytes 221188
  826.9 562.0 %all-gather.5.cloned.1.call-start = ((), (), s32[]{:S(2)}) async-start(), calls=%async_computation.1 | async-start | bytes 2949120 | tf_op jit(solution)/shard_map/all_gather | solution.py:289
  1063.7 4.6 copy-start.18
  1063.7 4.6 copy-start.39
  1365.9 209.7 %all-reduce.16.cloned.1.call-start = ((), (), s32[]{:S(2)}) async-start(), calls=%async_computation.3 | async-start | bytes 10223616 | tf_op jit(solution)/shard_map/psum | solution.py:295
  1369.0 5.4 copy-start.11
  1369.0 5.4 copy-start.41
  1374.4 3.5 copy-start.13
  1377.9 1.9 copy-start.6
  1381.6 5.5 copy-start.24
  1381.6 5.5 copy-start.25
  1381.6 5.5 copy-start.33
  1381.6 5.5 copy-start.34
  1387.1 8.4 copy-start.20
  1395.5 3.2 copy-start.5
  1401.4 3.5 copy-start.21
  1401.4 3.4 copy-start.27
  1575.6 6.7 copy-start.10
  1579.0 4.7 copy-start.1
Sparse Core Ops, SparseCore 0:
  608.4 23.0 all-gather.2
  660.4 125.5 all-reduce.17
  827.0 225.0 all-reduce.13
  1366.0 22.8 all-gather.4
  1393.9 181.6 all-reduce.15
where the time goes:
time: 1600 us; the launch traced here: 1590 us
  blocking collectives  833 us (52%)
  waiting for transfers between devices  494 us (31%)
  local copies, waits for them, and re-layouts  124 us (8%)
  matrix products  80 us (5%)
  other arithmetic  43.7 us (3%)
    unnamed x3, blocking collectives  793 us
    unnamed x6, waiting for transfers between devices  225 us
    psum x1, waiting for transfers between devices, local(): lax.psum((fc1_weight_grad, fc1_bias_grad, fc2_weight_grad, fc2_bias_grad,...  131 us
    psum x1, waiting for transfers between devices, local(): lax.psum(jnp.dot(activated, fc2_weight, preferred_element_type=jnp.float3...  125 us
    psum x1, blocking collectives, local(): lax.psum((fc1_weight_grad, fc1_bias_grad, fc2_weight_grad, fc2_bias_grad,...  39.9 us
  transfers between devices with their start and end apart: 5, of which 5 were waited for; matrix products, arithmetic and copies ran while one was open for 3% of the time, Pallas kernels for 0%

commit v1 on v0

v1 whole, which is shorter than its diff:
```python
import math

import jax
import jax.numpy as jnp
import numpy as np
from jax import lax
from jax.sharding import PartitionSpec as P

threshold = 0.01


def phase_angles(rows, columns, period):
    product = rows[:, None] * columns[None, :] % period
    return (np.float32(2.0 * math.pi / period) * product.astype(np.float32)).astype(np.float32)


def longitude_table(width, modes, padded):
    angles = phase_angles(np.arange(width), np.arange(modes), width)
    scale = np.float32(1.0 / math.sqrt(width))
    table = np.zeros((2, padded, width), np.float32)
    table[0, :modes] = (np.cos(angles) * scale).T
    table[1, :modes] = (-np.sin(angles) * scale).T
    return table.astype(jnp.bfloat16)


def latitude_table(period, own_rows, inner):
    angles = phase_angles(np.arange(period), np.arange(period), period)
    scale = np.float32(1.0 / math.sqrt(period))
    cosine = (np.cos(angles) * scale).reshape(period, -1, own_rows)
    sine = (np.sin(angles) * scale).reshape(period, -1, own_rows)
    owners = period // own_rows
    table = np.zeros((2, period, inner, owners, 2, own_rows, inner), np.float32)
    for index in range(inner):
        table[0, :, index, :, 0, :, index] = cosine
        table[0, :, index, :, 1, :, index] = sine
        table[1, :, index, :, 1, :, index] = cosine
        table[1, :, index, :, 0, :, index] = -sine
    return table.reshape(2 * period * inner, 2 * period * inner).astype(jnp.bfloat16)


def wide_dot(spec, left, right):
    return jnp.einsum(spec, left, right, preferred_element_type=jnp.float32)


def complex_apply(real_part, imag_part, weight):
    product = lambda left, right: wide_dot("mbc,bcd->mbd", left, right)
    real_out = product(real_part, weight[:, 0]) - product(imag_part, weight[:, 1])
    imag_out = product(imag_part, weight[:, 0]) + product(real_part, weight[:, 1])
    return real_out, imag_out


def complex_adjoint(grad_real, grad_imag, weight):
    product = lambda left, right: wide_dot("mbd,bcd->mbc", left, right)
    real_in = product(grad_real, weight[:, 0]) + product(grad_imag, weight[:, 1])
    imag_in = product(grad_imag, weight[:, 0]) - product(grad_real, weight[:, 1])
    return real_in, imag_in


def complex_weight_grads(real_part, imag_part, grad_real, grad_imag):
    outer = lambda left, right: wide_dot("mbc,mbd->bcd", left, right)
    weight_real = outer(real_part, grad_real) + outer(imag_part, grad_imag)
    weight_imag = outer(real_part, grad_imag) - outer(imag_part, grad_real)
    bias_real = jnp.sum(grad_real, 0, dtype=jnp.float32)
    bias_imag = jnp.sum(grad_imag, 0, dtype=jnp.float32)
    return jnp.stack([weight_real, weight_imag], 1), jnp.stack([bias_real, bias_imag], 1)


def layer_norm(values, gain, shift):
    centred = values - jnp.mean(values, -1, keepdims=True)
    variance = jnp.mean(centred * centred, -1, keepdims=True)
    inv_std = lax.rsqrt(variance + 1e-05)
    normal_hat = centred * inv_std
    return (normal_hat * gain + shift, normal_hat, inv_std)


def norm_backward(grad, normal_hat, inv_std, gain):
    scaled = grad * gain
    return inv_std * (
        scaled
        - jnp.mean(scaled, -1, keepdims=True)
        - normal_hat * jnp.mean(scaled * normal_hat, -1, keepdims=True)
    )


def shrink(values):
    return values - threshold * jnp.tanh(values / threshold)


def shrink_slope(values):
    bent = jnp.tanh(values / threshold)
    return bent * bent


def local(
    fields_in,
    norm1_gain,
    norm1_shift,
    spec_w1,
    spec_b1,
    spec_w2,
    spec_b2,
    norm2_gain,
    norm2_shift,
    fc1_weight,
    fc1_bias,
    fc2_weight,
    fc2_bias,
    out_grad,
):
    narrow = jnp.bfloat16
    fields, rows_here, width, channels = fields_in.shape
    sp_size, wa_size = lax.axis_size("sp"), lax.axis_size("wa")
    block = spec_w1.shape[2]
    blocks = channels // block
    modes = width // 2 + 1
    period = rows_here * sp_size
    each = -(-modes // (sp_size * wa_size))
    padded = each * sp_size * wa_size
    count = period * fields * each
    long_all = jnp.asarray(longitude_table(width, modes, padded))
    weights = np.where((np.arange(padded) == 0) | (2 * np.arange(padded) == width), 1.0, 2.0)
    long_back_all = jnp.asarray((longitude_table(width, modes, padded) * weights[None, :, None]).astype(narrow))
    lat = jnp.asarray(latitude_table(period, rows_here, fields * each))
    place = lax.axis_index("wa")
    pick = lambda table: lax.dynamic_slice_in_dim(
        table, place * (each * sp_size), each * sp_size, 1
    ).reshape(2, sp_size, each, width)
    long_own, long_back_own = pick(long_all), pick(long_back_all)
    long_all = long_all.reshape(2, wa_size, sp_size, each, width)
    long_back_all = long_back_all.reshape(2, wa_size, sp_size, each, width)
    w1 = lax.all_gather(spec_w1, "wa", axis=0, tiled=True)
    b1 = lax.all_gather(spec_b1, "wa", axis=0, tiled=True).astype(jnp.float32)
    w2 = lax.all_gather(spec_w2, "wa", axis=0, tiled=True)
    b2 = lax.all_gather(spec_b2, "wa", axis=0, tiled=True).astype(jnp.float32)

    def to_modes(rows_data, table):
        parts = wide_dot("xsjw,fhwc->sxhfjc", table, rows_data).astype(narrow)
        parts = parts.reshape(sp_size, -1, channels)
        return lax.all_to_all(parts, "sp", 0, 0, tiled=True).reshape(-1, channels)

    def to_rows(mode_data, table):
        parts = mode_data.astype(narrow).reshape(sp_size, -1, channels)
        parts = lax.all_to_all(parts, "sp", 0, 0, tiled=True)
        parts = lax.all_gather(parts, "wa", axis=0)
        parts = parts.reshape(wa_size, sp_size, 2, rows_here, fields, each, channels)
        return wide_dot("xasjw,asxhfjc->fhwc", table, parts)

    def halves(values):
        values = values.reshape(2, count, blocks, block)
        return values[0], values[1]

    def join(real_part, imag_part):
        return jnp.stack([real_part, imag_part]).reshape(2 * count, channels).astype(narrow)

    all_but_last = (0, 1, 2)
    input_wide = fields_in.astype(jnp.float32)
    normed_one, hat_one, inv_std_one = layer_norm(input_wide, norm1_gain, norm1_shift)
    columns = to_modes(normed_one.astype(narrow), long_own)
    spectrum = wide_dot("qh,hc->qc", lat, columns).astype(narrow)
    spec_real, spec_imag = halves(spectrum)
    one_real, one_imag = complex_apply(spec_real, spec_imag, w1)
    hid_real, real_pull = jax.vjp(jax.nn.gelu, one_real + b1[:, 0])
    hid_imag, imag_pull = jax.vjp(jax.nn.gelu, one_imag + b1[:, 1])
    hid_real = hid_real.astype(narrow)
    hid_imag = hid_imag.astype(narrow)
    two_real, two_imag = complex_apply(hid_real, hid_imag, w2)
    two_real = two_real + b2[:, 0]
    two_imag = two_imag + b2[:, 1]
    filtered = join(shrink(two_real), shrink(two_imag))
    filter_all = to_rows(wide_dot("qh,qc->hc", lat, filtered), long_back_all).astype(narrow)
    mixed = input_wide + filter_all.astype(jnp.float32)
    normed_two, hat_two, inv_std_two = layer_norm(mixed, norm2_gain, norm2_shift)
    normed_rows = normed_two.astype(narrow).reshape(-1, channels)
    hidden_pre = wide_dot("rd,de->re", normed_rows, fc1_weight) + fc1_bias.astype(jnp.float32)
    activated, gelu_pull = jax.vjp(jax.nn.gelu, hidden_pre)
    activated = activated.astype(narrow)
    grad_rows = out_grad.reshape(-1, channels)
    grad_act = wide_dot("rd,ed->re", grad_rows, fc2_weight)
    grad_hidden = gelu_pull(grad_act)[0].astype(narrow)
    grad_norm_part = wide_dot("re,de->rd", grad_hidden, fc1_weight)
    grad_norm_two = (
        lax.psum(grad_norm_part.astype(narrow), "wa").astype(jnp.float32).reshape(mixed.shape)
    )
    branch = lax.psum(wide_dot("re,ed->rd", activated, fc2_weight).astype(narrow), "wa")
    output = mixed + (branch.astype(jnp.float32) + fc2_bias.astype(jnp.float32)).reshape(mixed.shape)
    fc2_weight_grad = wide_dot("re,rd->ed", activated, grad_rows)
    fc2_bias_grad = jnp.sum(grad_rows, 0, dtype=jnp.float32)
    fc1_weight_grad = wide_dot("rd,re->de", normed_rows, grad_hidden)
    fc1_bias_grad = jnp.sum(grad_hidden, 0, dtype=jnp.float32)
    fc_sums = lax.psum((fc1_weight_grad.astype(narrow), fc2_weight_grad.astype(narrow)), "sp")
    norm2_gain_grad = jnp.sum(grad_norm_two * hat_two, all_but_last)
    norm2_shift_grad = jnp.sum(grad_norm_two, all_but_last)
    grad_mixed = out_grad.astype(jnp.float32) + norm_backward(
        grad_norm_two, hat_two, inv_std_two, norm2_gain
    )
    grad_columns = to_modes(grad_mixed.astype(narrow), long_back_own)
    grad_filtered = wide_dot("qh,hc->qc", lat, grad_columns)
    grad_out_real, grad_out_imag = halves(grad_filtered)
    grad_two_real = (grad_out_real * shrink_slope(two_real)).astype(narrow)
    grad_two_imag = (grad_out_imag * shrink_slope(two_imag)).astype(narrow)
    spec_w2_grad, spec_b2_grad = complex_weight_grads(
        hid_real, hid_imag, grad_two_real, grad_two_imag
    )
    grad_hid_real, grad_hid_imag = complex_adjoint(grad_two_real, grad_two_imag, w2)
    grad_one_real = real_pull(grad_hid_real)[0].astype(narrow)
    grad_one_imag = imag_pull(grad_hid_imag)[0].astype(narrow)
    spec_w1_grad, spec_b1_grad = complex_weight_grads(
        spec_real, spec_imag, grad_one_real, grad_one_imag
    )
    grad_spec_real, grad_spec_imag = complex_adjoint(grad_one_real, grad_one_imag, w1)
    grad_spectrum = join(grad_spec_real, grad_spec_imag)
    grad_norm_one = (
        to_rows(wide_dot("qh,qc->hc", lat, grad_spectrum), long_all)
        .astype(narrow)
        .astype(jnp.float32)
    )
    norm1_gain_grad = jnp.sum(grad_norm_one * hat_one, all_but_last)
    norm1_shift_grad = jnp.sum(grad_norm_one, all_but_last)
    fields_grad = grad_mixed + norm_backward(grad_norm_one, hat_one, inv_std_one, norm1_gain)
    own_blocks = blocks // wa_size
    spec_w1_grad, spec_w2_grad, spec_b1_grad, spec_b2_grad = [
        lax.dynamic_slice_in_dim(value, place * own_blocks, own_blocks, 0)
        for value in lax.psum(
            (spec_w1_grad, spec_w2_grad, spec_b1_grad, spec_b2_grad), ("sp", "wa")
        )
    ]
    sums = lax.psum(
        (
            fc1_bias_grad,
            fc2_bias_grad,
            norm1_gain_grad,
            norm1_shift_grad,
            norm2_gain_grad,
            norm2_shift_grad,
        ),
        "sp",
    )
    return (
        output,
        fields_grad,
        sums[2],
        sums[3],
        spec_w1_grad,
        spec_b1_grad,
        spec_w2_grad,
        spec_b2_grad,
        sums[4],
        sums[5],
        fc_sums[0].astype(jnp.float32),
        sums[0],
        fc_sums[1].astype(jnp.float32),
        sums[1],
    )


def solution(mesh):
    return jax.shard_map(
        local,
        mesh=mesh,
        in_specs=(
            P(None, "sp", None, None),
            P(),
            P(),
            P("wa", None, None, None),
            P("wa", None, None),
            P("wa", None, None, None),
            P("wa", None, None),
            P(),
            P(),
            P(None, "wa"),
            P("wa"),
            P("wa", None),
            P(),
            P(None, "sp", None, None),
        ),
        out_specs=(
            P(None, "sp", None, None),
            P(None, "sp", None, None),
            P(),
            P(),
            P("wa", None, None, None),
            P("wa", None, None),
            P("wa", None, None, None),
            P("wa", None, None),
            P(),
            P(),
            P(None, "wa"),
            P("wa"),
            P("wa", None),
            P(),
        ),
        check_vma=False,
    )
```

time: 1600 us -> 568 us (0.35)
  blocking collectives: 833 us -> 122 us
  waiting for transfers between devices: 494 us -> 254 us
  local copies, waits for them, and re-layouts: 124 us -> 59.5 us
  matrix products: 80 us -> 57.3 us
  starting transfers between devices: 0.61 us -> 17.6 us
    unnamed x3 -> x0, blocking collectives: 793 us -> none
    unnamed x6 -> x5, waiting for transfers between devices: 225 us -> 0.08 us
    psum x2 -> x3, waiting for transfers between devices: 256 us -> 213 us  [the longest x1 91.1 us: local(): lax.psum((spec_w1_grad, spec_w2_grad, spec_b1_grad, spec_b2_grad), ('sp',...]
    psum x1 -> x2, blocking collectives: 39.9 us -> 77.8 us  [the longest x1 40.1 us: local(): lax.psum((spec_w1_grad, spec_w2_grad, spec_b1_grad, spec_b2_grad), ('sp',...]
    add x5 -> x0, local copies, waits for them, and re-layouts: 37.6 us -> none  [the longest x2 18.2 us: modes_from_rows(): first + jnp.einsum('qh,hfkc->qfkc', sine, swap_forward(rows_data), prefer...]
    all_gather x0 -> x4, blocking collectives: none -> 23.7 us  [the longest x1 7.03 us: local(): w1 = lax.all_gather(spec_w1, 'wa', axis=0, tiled=True)]
    dot_general x46 -> x38, matrix products: 80 us -> 57.3 us  [wide_dot(): return jnp.einsum(spec, left, right, preferred_element_type=jnp.float32)]
    all_to_all x0 -> x1, blocking collectives: none -> 20.2 us  [to_rows(): parts = lax.all_to_all(parts, 'sp', 0, 0, tiled=True)]
  transfers between devices with their start and end apart: 5 -> 8, of which waited for: 5 -> 7; matrix products, arithmetic and copies ran while one was open for 3% -> 12% of each run, Pallas kernels for 0% -> 0%
where the time goes in v1:
time: 568 us; the launch traced here: 560 us
  waiting for transfers between devices  254 us (45%)
  blocking collectives  122 us (21%)
  local copies, waits for them, and re-layouts  59.5 us (10%)
  matrix products  57.3 us (10%)
  other arithmetic  34.3 us (6%)
  starting transfers between devices  17.6 us (3%)
  between operations  15.1 us (3%)
    psum x1, waiting for transfers between devices, local(): lax.psum((spec_w1_grad, spec_w2_grad, spec_b1_grad, spec_b2_grad), ('sp',...  91.1 us
    psum x1, waiting for transfers between devices, local(): lax.psum(grad_norm_part.astype(narrow), 'wa').astype(jnp.float32)  71.1 us
    dot_general x38, matrix products, wide_dot(): return jnp.einsum(spec, left, right, preferred_element_type=jnp.float32)  57.3 us
    psum x1, waiting for transfers between devices, local(): lax.psum((fc1_weight_grad.astype(narrow), fc2_weight_grad.astype(narrow))...  51.1 us
    psum x1, blocking collectives, local(): lax.psum((spec_w1_grad, spec_w2_grad, spec_b1_grad, spec_b2_grad), ('sp',...  40.1 us
    psum x1, blocking collectives, local(): lax.psum((fc1_bias_grad, fc2_bias_grad, norm1_gain_grad, norm1_shift_grad...  37.7 us
    all_gather x2, waiting for transfers between devices, to_rows(): parts = lax.all_gather(parts, 'wa', axis=0)  25.6 us
    all_to_all x1, blocking collectives, to_rows(): parts = lax.all_to_all(parts, 'sp', 0, 0, tiled=True)  20.2 us
  transfers between devices with their start and end apart: 8, of which 7 were waited for; matrix products, arithmetic and copies ran while one was open for 12% of the time, Pallas kernels for 0%

profile of v1, /device:TPU:0, one launch (start us, length us, event | category | flops | bytes accessed | tf_op | source)
XLA Modules:
  0.0 559.9 jit_solution(10528512096109072430)
XLA Ops:
  7.2 1.9 convert_reduce_fusion
  9.1 2.1 fusion.14
  14.0 7.3 %all-to-all-start = ((bf16[8,36,768]{2,1,0:T(8,128)(2,1)}), bf16[8,36,768]{2,1,0:T(8,128)(2,1)}, u32[]{:S(2)}, u32[]{:S(2)}) async-start(bf16[8,36,768]{2,1,0:T(8,128)(2,1)} %copy.90), calls=%async_computation | async-start | bytes 983040 | tf_op jit(solution)/shard_map/all_to_all | solution.py:139
  21.3 5.1 all_gather.25
  26.4 5.1 all_gather.27
  31.5 6.5 %all_gather.26 = bf16[8,2,96,96]{3,2,0,1:T(8,128)(2,1)S(1)} all-gather(bf16[2,2,96,96]{3,2,0,1:T(8,128)(2,1)S(1)} %copy.94), channel_id=1, replica_groups=mesh['sp'=8,'wa'=4] {'wa'}, dimensions={0}, use_global_device_ids=true | all-gather | bytes 368640 | tf_op jit(solution)/shard_map/all_gather | solution.py:133
  38.0 7.0 %all_gather.24 = bf16[8,2,96,96]{3,2,0,1:T(8,128)(2,1)} all-gather(bf16[2,2,96,96]{3,2,0,1:T(8,128)(2,1)S(1)} %copy.91), channel_id=1, replica_groups=mesh['sp'=8,'wa'=4] {'wa'}, dimensions={0}, use_global_device_ids=true | all-gather | bytes 368640 | tf_op jit(solution)/shard_map/all_gather | solution.py:131
  45.1 1.9 reshape.148
  47.0 1.4 fusion.60
  49.1 1.3 squeeze.16
  50.5 2.1 squeeze.18
  52.6 1.4 fusion.89
  54.0 1.2 fusion.97
  55.2 2.2 multiply_convert_fusion.1
  62.3 2.3 convert_element_type.160
  64.6 2.3 fusion.58
  66.9 1.9 reshape.149
  68.8 20.2 %all_to_all.20 = bf16[8,36,768]{2,1,0:T(8,128)(2,1)S(1)} all-to-all(bf16[8,36,768]{2,1,0:T(8,128)(2,1)} %reshape.149), channel_id=1, replica_groups=mesh['sp'=8,'wa'=4] {'sp'}, dimensions={0} | all-to-all | bytes 884736 | tf_op jit(solution)/shard_map/all_to_all | solution.py:143
  90.7 2.8 copy.100
  93.5 3.6 reshape.154
  97.1 5.0 fusion.117
  102.1 7.8 %all-gather.5.cloned.1.call-done = bf16[32,36,768]{2,0,1:T(8,128)(2,1)} async-done(((bf16[8,36,768]{2,0,1:T(8,128)(2,1)}), bf16[32,36,768]{2,0,1:T(8,128)(2,1)}) %all-gather.5.cloned.1.call-update) | async-done | bytes 1769488 | tf_op jit(solution)/shard_map/all_gather | solution.py:144
  109.9 2.1 fusion.28
  113.6 2.0 add_convert_fusion
  115.6 3.6 reshape.152
  119.2 6.7 %convert_reduce_fusion.3 = (f32[768]{0:T(1024)}, bf16[1080,768]{1,0:T(8,128)(2,1)S(1)}, f32[1080,768]{1,0:T(8,128)S(1)}) fusion(f32[1080,768]{1,0:T(8,128)} %fusion.117, f32[768]{0:T(1024)} %convert_element_type.167, bf16[1080,768]{1,0:T(8,128)(2,1)} %reshape.152, bf16[768,768]{1,0:T(8,128)(2,1)S(1)} %copy-done), kind=kOutput, calls=%fused_computation.42 | convolution fusion | flops 1293096192 | bytes 11139072 | tf_op jit(solution)/shard_map/rd,de->re/dot_general | solution.py:42
  125.9 2.8 convolution_convert_fusion
  128.7 3.3 convolution_convert_fusion.1
  132.8 71.1 %all-reduce.13.cloned.1.call-done = (bf16[1080,768]{1,0:T(8,128)(2,1)}, bf16[1080,768]{1,0:T(8,128)(2,1)}) async-done(((bf16[1080,768]{1,0:T(8,128)(2,1)}, bf16[1080,768]{1,0:T(8,128)(2,1)}), (bf16[1080,768]{1,0:T(8,128)(2,1)}, bf16[1080,768]{1,0:T(8,128)(2,1)})) %all-reduce.13.cloned.1.call-update) | async-done | bytes 3317776 | tf_op jit(solution)/shard_map/psum | solution.py:182
  203.9 2.6 convert_reduce_fusion.4
  206.5 3.7 reshape.155
  210.3 4.2 multiply_reduce_fusion
  214.8 2.0 fusion.55
  217.7 5.7 %all-to-all-start.2 = ((bf16[8,36,768]{2,1,0:T(8,128)(2,1)}), bf16[8,36,768]{2,1,0:T(8,128)(2,1)S(1)}, u32[]{:S(2)}, u32[]{:S(2)}) async-start(bf16[8,36,768]{2,1,0:T(8,128)(2,1)} %copy.104), calls=%async_computation.2 | async-start | bytes 983040 | tf_op jit(solution)/shard_map/all_to_all | solution.py:139
  223.5 4.9 convolution_convert_fusion.3
  228.4 3.1 convolution_convert_fusion.2
  231.5 5.7 %all-to-all-done.2 = bf16[8,36,768]{2,1,0:T(8,128)(2,1)S(1)} async-done(((bf16[8,36,768]{2,1,0:T(8,128)(2,1)}), bf16[8,36,768]{2,1,0:T(8,128)(2,1)S(1)}, u32[]{:S(2)}, u32[]{:S(2)}) %all-to-all-start.2) | async-done | bytes 442400 | tf_op jit(solution)/shard_map/all_to_all | solution.py:139
  238.7 2.1 squeeze.42
  240.8 2.0 convert_reduce_fusion.6
  243.9 2.1 squeeze.43
  246.0 1.9 convert_reduce_fusion.5
  248.2 2.6 convert_reduce_fusion.7
  254.4 1.6 convert_element_type.183
  256.0 2.1 fusion.59
  258.1 1.9 reshape.159
  260.0 4.3 all-to-all-start.3
  264.7 1.3 fusion.64
  266.1 1.3 fusion.120
  271.2 9.7 %all-to-all-done.3 = bf16[8,36,768]{2,1,0:T(8,128)(2,1)} async-done(((bf16[8,36,768]{2,1,0:T(8,128)(2,1)}), bf16[8,36,768]{2,1,0:T(8,128)(2,1)}, u32[]{:S(2)}, u32[]{:S(2)}) %all-to-all-start.3) | async-done | bytes 442400 | tf_op jit(solution)/shard_map/all_to_all | solution.py:143
  280.9 1.9 copy.108
  282.8 3.4 convert_add_fusion.2
  286.2 4.6 reshape.153
  290.8 51.1 %all-reduce.11.cloned.1.call-done = (bf16[768,768]{1,0:T(8,128)(2,1)}, bf16[768,768]{1,0:T(8,128)(2,1)}) async-done(((bf16[768,768]{1,0:T(8,128)(2,1)}, bf16[768,768]{1,0:T(8,128)(2,1)}), (bf16[768,768]{1,0:T(8,128)(2,1)}, bf16[768,768]{1,0:T(8,128)(2,1)})) %all-reduce.11.cloned.1.call-update) | async-done | bytes 2359312 | tf_op jit(solution)/shard_map/psum | solution.py:190
  342.0 2.9 convert_element_type.194
  344.9 1.6 convert_element_type.197
  346.5 40.1 %all-reduce = (f32[8,2,96]{2,1,0:T(2,128)S(1)}, f32[8,2,96]{2,1,0:T(2,128)S(1)}) all-reduce(f32[8,2,96]{2,1,0:T(2,128)S(1)} %pad_maximum_fusion.4, f32[8,2,96]{2,1,0:T(2,128)S(1)} %pad_maximum_fusion.5), channel_id=1, replica_groups=mesh['sp'=8,'wa'=4] {'sp','wa'}, use_global_device_ids=true, to_apply=%region_17.0 | all-reduce | flops 3072 | bytes 24576 | tf_op jit(solution)/shard_map/psum | solution.py:223
  387.8 91.1 %all-reduce.9.cloned.1.call-done = (f32[8,2,96,96]{3,2,0,1:T(8,128)}, f32[8,2,96,96]{3,2,0,1:T(8,128)}) async-done(((f32[8,2,96,96]{3,2,0,1:T(8,128)}, f32[8,2,96,96]{3,2,0,1:T(8,128)}), (f32[8,2,96,96]{3,2,0,1:T(8,128)}, f32[8,2,96,96]{3,2,0,1:T(8,128)})) %all-reduce.9.cloned.1.call-update) | async-done | bytes 1179664 | tf_op jit(solution)/shard_map/psum | solution.py:223
  482.1 17.8 %all-gather.7.cloned.1.call-done = bf16[32,36,768]{2,0,1:T(8,128)(2,1)} async-done(((bf16[8,36,768]{2,0,1:T(8,128)(2,1)}), bf16[32,36,768]{2,0,1:T(8,128)(2,1)}) %all-gather.7.cloned.1.call-update) | async-done | bytes 1769488 | tf_op jit(solution)/shard_map/all_gather | solution.py:144
  500.0 2.3 fusion.26
  502.8 1.9 fusion.16
  505.2 3.1 fusion.13
  508.3 3.4 copy.115
  511.8 3.4 copy.114
  515.2 37.7 %all-reduce.2 = (f32[768]{0:T(1024)}, f32[768]{0:T(1024)}, f32[768]{0:T(1024)}, f32[768]{0:T(1024)}, f32[768]{0:T(1024)}, /*index=5*/f32[768]{0:T(1024)}) all-reduce(f32[768]{0:T(1024)S(1)} %get-tuple-element.58, f32[768]{0:T(1024)S(1)} %get-tuple-element.83, f32[768]{0:T(1024)S(1)} %copy-done.45, ...), channel_id=1, replica_groups=mesh['sp'=8,'wa'=4] {'sp'}, use_global_device_ids=true, to_apply=%region_11.0 | all-reduce | flops 4608 | bytes 36864 | tf_op jit(solution)/shard_map/psum | solution.py:227
  (198 shorter events, 29.7 us)
Async XLA Ops:
  7.2 112.0 %copy-start = (bf16[768,768]{1,0:T(8,128)(2,1)S(1)}, bf16[768,768]{1,0:T(8,128)(2,1)}, u32[]{:S(2)}) copy-start(bf16[768,768]{1,0:T(8,128)(2,1)} %param.26) | copy-start | bytes 3538948
  7.2 4.8 copy-start.2
  7.2 4.8 copy-start.46
  7.2 4.8 copy-start.57
  11.2 2.7 copy-start.35
  12.0 9.2 %copy-start.33 = (bf16[2,2,96,96]{3,2,1,0:T(8,128)(2,1)S(1)}, bf16[2,2,96,96]{3,2,1,0:T(8,128)(2,1)}, u32[]{:S(2)}) copy-start(bf16[2,2,96,96]{3,2,1,0:T(8,128)(2,1)} %param.20) | copy-start | bytes 221188
  12.1 9.2 %copy-start.34 = (bf16[2,2,96,96]{3,2,1,0:T(8,128)(2,1)S(1)}, bf16[2,2,96,96]{3,2,1,0:T(8,128)(2,1)}, u32[]{:S(2)}) copy-start(bf16[2,2,96,96]{3,2,1,0:T(8,128)(2,1)} %param.22) | copy-start | bytes 221188
  12.1 9.3 %copy-start.54 = (bf16[2,2,96]{2,1,0:T(2,128)(2,1)S(1)}, bf16[2,2,96]{2,1,0:T(2,128)(2,1)}, u32[]{:S(2)}) copy-start(bf16[2,2,96]{2,1,0:T(2,128)(2,1)} %param.21) | copy-start | bytes 2308
  12.1 14.3 %copy-start.55 = (bf16[2,2,96]{2,1,0:T(2,128)(2,1)S(1)}, bf16[2,2,96]{2,1,0:T(2,128)(2,1)}, u32[]{:S(2)}) copy-start(bf16[2,2,96]{2,1,0:T(2,128)(2,1)} %param.23) | copy-start | bytes 2308
  13.1 33.9 %copy-start.27 = (bf16[288,288]{1,0:T(8,128)(2,1)S(1)}, bf16[288,288]{1,0:T(8,128)(2,1)}, u32[]{:S(2)}) copy-start(bf16[288,288]{1,0:T(8,128)(2,1)} %constant.60.clone) | copy-start | bytes 497668
  14.0 31.1 %all-to-all-start = ((bf16[8,36,768]{2,1,0:T(8,128)(2,1)}), bf16[8,36,768]{2,1,0:T(8,128)(2,1)}, u32[]{:S(2)}, u32[]{:S(2)}) async-start(bf16[8,36,768]{2,1,0:T(8,128)(2,1)} %copy.90), calls=%async_computation | async-start | bytes 983040 | tf_op jit(solution)/shard_map/all_to_all | solution.py:139
  21.2 88.6 %all-gather.5.cloned.1.call-start = ((), (), s32[]{:S(2)}) async-start(), calls=%async_computation.4 | async-start | bytes 2211840 | tf_op jit(solution)/shard_map/all_gather | solution.py:144
  50.4 4.7 copy-start.18
  52.6 5.1 copy-start.11
  52.6 5.1 copy-start.20
  61.3 28.8 %copy-start.52 = (bf16[768]{0:T(1024)(128)(2,1)S(1)}, bf16[768]{0:T(1024)(128)(2,1)}, u32[]{:S(2)}) copy-start(bf16[768]{0:T(1024)(128)(2,1)} %param.27) | copy-start | bytes 4612
  89.9 114.0 %all-reduce.13.cloned.1.call-start = ((), (), s32[]{:S(2)}) async-start(), calls=%async_computation.8 | async-start | bytes 6635520 | tf_op jit(solution)/shard_map/psum | solution.py:182
  112.0 1.6 copy-start.37
  112.0 1.6 copy-start.51
  125.9 2.8 copy-start.59
  125.9 2.8 copy-start.60
  125.9 2.8 copy-start.56
  210.3 4.3 copy-start.38
  210.3 4.3 copy-start.4
  210.3 4.3 copy-start.6
  210.3 4.5 copy-start.9
  214.6 2.2 copy-start.40
  217.7 19.5 %all-to-all-start.2 = ((bf16[8,36,768]{2,1,0:T(8,128)(2,1)}), bf16[8,36,768]{2,1,0:T(8,128)(2,1)S(1)}, u32[]{:S(2)}, u32[]{:S(2)}) async-start(bf16[8,36,768]{2,1,0:T(8,128)(2,1)} %copy.104), calls=%async_computation.2 | async-start | bytes 983040 | tf_op jit(solution)/shard_map/all_to_all | solution.py:139
  223.5 118.5 %all-reduce.11.cloned.1.call-start = ((), (), s32[]{:S(2)}) async-start(), calls=%async_computation.7 | async-start | bytes 4718592 | tf_op jit(solution)/shard_map/psum | solution.py:190
  223.5 4.9 copy-start.29
  223.5 4.9 copy-start.61
  231.5 5.8 %copy-start.28 = (bf16[288,288]{1,0:T(8,128)(2,1)S(1)}, bf16[288,288]{1,0:T(8,128)(2,1)}, u32[]{:S(2)}) copy-start(bf16[288,288]{1,0:T(8,128)(2,1)} %constant.60.clone) | copy-start | bytes 497668
  237.7 8.3 %copy-start.14 = (f32[144,8,96]{2,0,1:T(8,128)S(1)}, f32[144,8,96]{2,0,1:T(8,128)}, u32[]{:S(2)}) copy-start(f32[144,8,96]{2,0,1:T(8,128)} %copy-done.13) | copy-start | bytes 1327108
  246.0 4.7 copy-start.12
  247.9 4.3 copy-start.24
  247.9 3.1 copy-start.31
  247.9 3.1 copy-start.58
  253.2 11.1 %copy-start.17 = (bf16[144,8,96]{2,0,1:T(8,128)(2,1)S(1)}, bf16[144,8,96]{2,0,1:T(8,128)(2,1)}, u32[]{:S(2)}) copy-start(bf16[144,8,96]{2,0,1:T(8,128)(2,1)} %copy-done.16) | copy-start | bytes 663556
  253.3 11.1 %copy-start.23 = (bf16[144,8,96]{2,0,1:T(8,128)(2,1)S(1)}, bf16[144,8,96]{2,0,1:T(8,128)(2,1)}, u32[]{:S(2)}) copy-start(bf16[144,8,96]{2,0,1:T(8,128)(2,1)} %copy-done.22) | copy-start | bytes 663556
  258.1 9.6 %copy-start.19 = (bf16[144,8,96]{2,1,0:T(8,128)(2,1)S(1)}, bf16[144,8,96]{2,1,0:T(8,128)(2,1)}, u32[]{:S(2)}) copy-start(bf16[144,8,96]{2,1,0:T(8,128)(2,1)} %copy-done.18) | copy-start | bytes 663556
  260.0 8.1 %copy-start.21 = (bf16[144,8,96]{2,1,0:T(8,128)(2,1)S(1)}, bf16[144,8,96]{2,1,0:T(8,128)(2,1)}, u32[]{:S(2)}) copy-start(bf16[144,8,96]{2,1,0:T(8,128)(2,1)} %squeeze.18) | copy-start | bytes 663556
  260.0 20.8 %all-to-all-start.3 = ((bf16[8,36,768]{2,1,0:T(8,128)(2,1)}), bf16[8,36,768]{2,1,0:T(8,128)(2,1)}, u32[]{:S(2)}, u32[]{:S(2)}) async-start(bf16[8,36,768]{2,1,0:T(8,128)(2,1)} %reshape.159), calls=%async_computation.3 | async-start | bytes 983040 | tf_op jit(solution)/shard_map/all_to_all | solution.py:143
  264.3 214.6 %all-reduce.9.cloned.1.call-start = ((), (), s32[]{:S(2)}) async-start(), calls=%async_computation.6 | async-start | bytes 3145728 | tf_op jit(solution)/shard_map/psum | solution.py:223
  264.4 3.7 copy-start.26
  269.2 13.6 %copy-start.53 = (bf16[768]{0:T(1024)(128)(2,1)S(1)}, bf16[768]{0:T(1024)(128)(2,1)}, u32[]{:S(2)}) copy-start(bf16[768]{0:T(1024)(128)(2,1)} %param.29) | copy-start | bytes 4612
  271.1 228.8 %all-gather.7.cloned.1.call-start = ((), (), s32[]{:S(2)}) async-start(), calls=%async_computation.5 | async-start | bytes 2211840 | tf_op jit(solution)/shard_map/all_gather | solution.py:144
  341.9 3.0 copy-start.30
  341.9 4.5 copy-start.43
  341.9 4.5 copy-start.44
  341.9 4.6 copy-start.49
  341.9 4.6 copy-start.50
  344.9 155.1 %copy-start.32 = (bf16[2,4,8,3,180,1,1]{4,2,3,1,6,5,0:T(8,128)(2,1)S(1)}, bf16[2,4,8,3,180,1,1]{4,2,3,1,6,5,0:T(8,128)(2,1)}, u32[]{:S(2)}) copy-start(bf16[2,4,8,3,180,1,1]{4,2,3,1,6,5,0:T(8,128)(2,1)} %constant.70) | copy-start | bytes 207364
  500.0 2.8 copy-start.36
  500.0 2.8 copy-start.47
  500.0 4.7 copy-start.8
  502.3 2.4 copy-start.5
  502.3 2.5 copy-start.7
  502.3 2.9 copy-start.10
  502.3 2.9 copy-start.39
  502.3 2.9 copy-start.41
  511.8 41.2 %copy-start.1 = (bf16[768,768]{1,0:T(8,128)(2,1)S(1)}, bf16[768,768]{1,0:T(8,128)(2,1)}, u32[]{:S(2)}) copy-start(bf16[768,768]{1,0:T(8,128)(2,1)} %param.26) | copy-start | bytes 3538948
  511.8 3.4 copy-start.42
  511.8 3.4 copy-start.45
  511.8 3.4 copy-start.48
  (6 other events, 5.4 us)
Sparse Core Ops, SparseCore 0:
  90.0 19.8 all-gather.4
  132.2 71.6 all-reduce.12
  231.6 110.2 all-reduce.10
  347.3 131.5 all-reduce.8
  480.3 19.6 all-gather.6
